TPU v7x, 256 devices: a whole 4x4x8 slice. The times are simulated.
256 devices in a mesh: wide: 32 (over z, x), narrow: 8 (over y, core).
Axes of the slice: x: 4, y: 4, z: 8, core: 2. Of those that a mesh axis runs over, the one named last changes fastest.
Arguments:
- tokens: bfloat16 [32, 9216, 1280], P('wide', 'narrow'), may hold values from -64 to 64
- slot_keys: bfloat16 [1280, 256], P(None, 'wide'), may hold values from -2 to 2
- w_in: bfloat16 [64, 1280, 5120], P('wide', None, 'narrow'), may hold values from -0.15625 to 0.15625
- b_in: bfloat16 [64, 5120], P('wide', 'narrow'), may hold values from -3 to 3
- w_out: bfloat16 [64, 5120, 1280], P('wide', 'narrow'), may hold values from -0.078125 to 0.078125
- b_out: bfloat16 [64, 1280], P('wide'), may hold values from -1.1953125 to 1.1953125
Outputs:
- mixed_out: bfloat16 [32, 9216, 1280], P('wide', 'narrow')
All inputs are finite; a program needn't handle non-finite values.
Results may differ from a plain program's by a relative error of at most 0.0064.
Values may be sent and summed in bfloat16 or wider, within the bound.
A program may use at most 64 MiB of HBM per device.

v0:
```python
import jax
import jax.numpy as jnp
from jax import lax
from jax.sharding import PartitionSpec as P


def on_device(tokens, slot_keys, w_in, b_in, w_out, b_out):
    token_rows = tokens[0]
    wide_count = lax.axis_size("wide")
    per_owner = slot_keys.shape[1]
    model_width = token_rows.shape[1]
    logits = jnp.dot(
        token_rows,
        lax.all_gather(slot_keys, "wide", axis=1, tiled=True),
        preferred_element_type=jnp.float32,
    )
    column_top = lax.pmax(jnp.max(logits, axis=0), "narrow")
    spread = jnp.exp(logits - column_top[None, :])
    totals = jnp.sum(spread, axis=0).reshape(wide_count, per_owner)
    slot_sums = lax.dot_general(
        spread.astype(jnp.bfloat16),
        token_rows,
        (((0,), (0,)), ((), ())),
        preferred_element_type=jnp.float32,
    ).reshape(wide_count, per_owner, model_width)
    summed, summed_totals = lax.psum((slot_sums, totals), "narrow")
    slot_inputs = (summed / summed_totals[:, :, None]).astype(jnp.bfloat16)
    arrived = lax.all_to_all(slot_inputs, "wide", split_axis=0, concat_axis=0, tiled=True)
    clip_count = arrived.shape[0]
    expert_count = w_in.shape[0]
    grouped = arrived.reshape(clip_count, expert_count, per_owner // expert_count, model_width)
    hidden = jnp.einsum("cesd,edf->cesf", grouped, w_in, preferred_element_type=jnp.float32)
    hidden = jax.nn.gelu(
        hidden + b_in[None, :, None, :].astype(jnp.float32), approximate=True
    ).astype(jnp.bfloat16)
    partial_out = jnp.einsum("cesf,efd->cesd", hidden, w_out, preferred_element_type=jnp.float32)
    partial_out = partial_out.reshape(clip_count, per_owner, model_width)
    bias_rows = jnp.repeat(b_out.astype(jnp.float32), per_owner // expert_count, axis=0)
    expert_sum = lax.psum(partial_out, "narrow")
    slot_outputs = (expert_sum + bias_rows[None]).astype(jnp.bfloat16)
    returned = lax.all_to_all(slot_outputs, "wide", split_axis=0, concat_axis=0, tiled=True)
    slot_outputs_all = returned.reshape(-1, model_width)
    row_top = jnp.max(logits, axis=1, keepdims=True)
    row_spread = jnp.exp(logits - row_top)
    row_totals = jnp.sum(row_spread, axis=1, keepdims=True)
    summed_rows = jnp.dot(
        row_spread.astype(jnp.bfloat16), slot_outputs_all, preferred_element_type=jnp.float32
    )
    mixed_out = (summed_rows / row_totals).astype(jnp.bfloat16)
    return mixed_out[None]


def solution(mesh):
    in_specs = (
        P("wide", "narrow", None),
        P(None, "wide"),
        P("wide", None, "narrow"),
        P("wide", "narrow"),
        P("wide", "narrow", None),
        P("wide", None),
    )
    out_specs = P("wide", "narrow", None)
    return jax.shard_map(
        on_device, mesh=mesh, in_specs=in_specs, out_specs=out_specs, check_vma=False
    )
```

profile of v0, /device:TPU:1, one launch (start us, length us, event | category | flops | bytes accessed | tf_op | source)
XLA Modules:
  0.0 285.8 jit_solution(7177636967835935330)
XLA Ops:
  6.5 0.0 copy-start
  6.5 0.0 all-reduce.3.cloned.1.call-start
  6.5 42.5 %all_gather.3 = bf16[1280,256]{0,1:T(8,128)(2,1)S(1)} all-gather(bf16[1280,8]{0,1:T(8,128)(2,1)} %param.7), channel_id=1, replica_groups=mesh['wide'=32,'narrow'=8] {'wide'}, dimensions={1}, use_global_device_ids=true | all-gather | bytes 675840 | tf_op jit(solution)/shard_map/all_gather | solution.py:14
  49.0 3.9 %fusion.46 = (f32[256]{0:T(256)S(1)}, f32[1152]{0:T(1024)S(1)}, f32[1152,256]{0,1:T(8,128)}) fusion(bf16[1280,256]{0,1:T(8,128)(2,1)S(1)} %all_gather.3, bf16[1,1152,1280]{2,1,0:T(8,128)(2,1)} %param.6), kind=kOutput, calls=%fused_computation.40 | convolution fusion | flops 755563136 | bytes 4789760 | tf_op jit(solution)/shard_map/dot_general | solution.py:12
  53.0 24.1 %pmax.7 = f32[256]{0:T(256)S(1)} all-reduce(f32[256]{0:T(256)S(1)} %get-tuple-element.7), channel_id=1, replica_groups=mesh['wide'=32,'narrow'=8] {'narrow'}, use_global_device_ids=true, to_apply=%region_2.0 | all-reduce | flops 256 | bytes 2048 | tf_op jit(solution)/shard_map/pmax | solution.py:17
  77.1 4.4 %fusion.6 = f32[32,8,1280]{2,1,0:T(8,128)} fusion(bf16[1,1152,1280]{2,1,0:T(8,128)(2,1)} %param.6, f32[1152,256]{0,1:T(8,128)} %get-tuple-element.9, f32[256]{0:T(256)S(1)} %pmax.7), kind=kOutput, calls=%fused_computation.7 | convolution fusion | flops 755564544 | bytes 5440512 | tf_op jit(solution)/shard_map/dot_general | solution.py:20
  81.5 0.0 all-reduce.3.cloned.1.call-update
  81.5 1.7 fusion.18
  83.2 0.1 reshape.21
  83.2 20.5 %psum.22 = f32[32,8]{1,0:T(8,128)S(1)} all-reduce(f32[32,8]{1,0:T(8,128)S(1)} %reshape.21), channel_id=1, replica_groups=mesh['wide'=32,'narrow'=8] {'narrow'}, use_global_device_ids=true, to_apply=%region_5.0 | all-reduce | flops 256 | bytes 2048 | tf_op jit(solution)/shard_map/psum | solution.py:26
  103.7 0.0 copy-start.3
  103.7 39.5 %all-reduce.3.cloned.1.call-done = f32[32,8,1280]{2,1,0:T(8,128)} async-done(((f32[32,8,1280]{2,1,0:T(8,128)}), f32[32,8,1280]{2,1,0:T(8,128)}) %all-reduce.3.cloned.1.call-update) | async-done | bytes 1310736 | tf_op jit(solution)/shard_map/psum | solution.py:26
  143.2 2.3 divide_convert_fusion
  145.5 9.7 %all-to-all-start = ((bf16[32,8,1280]{2,1,0:T(8,128)(2,1)}), bf16[32,8,1280]{2,1,0:T(8,128)(2,1)}, u32[]{:S(2)}, u32[]{:S(2)}) async-start(bf16[32,8,1280]{2,1,0:T(8,128)(2,1)} %divide_convert_fusion), calls=%async_computation | async-start | bytes 1310720 | tf_op jit(solution)/shard_map/all_to_all | solution.py:28
  155.2 0.0 all-reduce.5.cloned.1.call-start
  155.2 0.0 copy-done.3
  155.3 16.4 %all-to-all-done = bf16[32,8,1280]{2,1,0:T(8,128)(2,1)} async-done(((bf16[32,8,1280]{2,1,0:T(8,128)(2,1)}), bf16[32,8,1280]{2,1,0:T(8,128)(2,1)}, u32[]{:S(2)}, u32[]{:S(2)}) %all-to-all-start) | async-done | bytes 655392 | tf_op jit(solution)/shard_map/all_to_all | solution.py:28
  171.6 2.1 copy.12
  173.7 0.0 copy-done
  173.7 4.5 %fusion.2 = f32[2,32,4,1280]{3,1,2,0:T(8,128)} fusion(bf16[2,640,1280]{2,1,0:T(8,128)(2,1)S(1)} %copy-done, bf16[32,2,4,1280]{3,0,2,1:T(8,128)(2,1)} %bitcast.53, bf16[2,1280,640]{2,1,0:T(8,128)(2,1)} %param.8, f32[2,640]{1,0:T(2,128)S(1)} %convert_element_type.33), kind=kOutput, calls=%fused_computation.3 | convolution fusion | flops 840499200 | bytes 8524800 | tf_op jit(solution)/shard_map/cesf,efd->cesd/dot_general | solution.py:36
  178.2 3.2 %copy.9 = f32[32,8,1280]{2,1,0:T(8,128)} copy(f32[32,8,1280]{2,0,1:T(8,128)} %bitcast.52) | data formatting | bytes 2621440 | tf_op jit(solution)/shard_map/reshape | solution.py:37
  181.3 0.0 copy-start.2
  181.3 0.0 all-reduce.5.cloned.1.call-update
  181.4 0.7 copy-done.2
  182.0 67.0 %all-reduce.5.cloned.1.call-done = f32[32,8,1280]{2,1,0:T(8,128)} async-done(((f32[32,8,1280]{2,1,0:T(8,128)}), f32[32,8,1280]{2,1,0:T(8,128)}) %all-reduce.5.cloned.1.call-update) | async-done | bytes 1310736 | tf_op jit(solution)/shard_map/psum | solution.py:39
  249.1 0.0 copy-start.1
  249.1 1.5 add_convert_fusion
  250.6 25.8 %all_to_all.10 = bf16[32,8,1280]{2,1,0:T(8,128)(2,1)S(1)} all-to-all(bf16[32,8,1280]{2,1,0:T(8,128)(2,1)S(1)} %add_convert_fusion), channel_id=1, replica_groups=mesh['wide'=32,'narrow'=8] {'wide'}, dimensions={0} | all-to-all | bytes 1310720 | tf_op jit(solution)/shard_map/all_to_all | solution.py:41
  276.3 0.0 copy-done.1
  276.3 2.6 fusion.1
  (3 shorter events, 0.0 us)
Async XLA Ops:
  6.5 167.2 %copy-start = (bf16[2,640,1280]{2,1,0:T(8,128)(2,1)S(1)}, bf16[2,640,1280]{2,1,0:T(8,128)(2,1)}, u32[]{:S(2)}) copy-start(bf16[2,640,1280]{2,1,0:T(8,128)(2,1)} %param.10) | copy-start | bytes 9830404
  6.5 136.7 %all-reduce.3.cloned.1.call-start = ((), (), s32[]{:S(2)}) async-start(), calls=%async_computation.2 | async-start | bytes 2621440 | tf_op jit(solution)/shard_map/psum | solution.py:26
  103.7 51.5 %copy-start.3 = (bf16[2,640]{1,0:T(2,128)(2,1)S(1)}, bf16[2,640]{1,0:T(2,128)(2,1)}, u32[]{:S(2)}) copy-start(bf16[2,640]{1,0:T(2,128)(2,1)} %param.9) | copy-start | bytes 7684
  145.5 26.1 %all-to-all-start = ((bf16[32,8,1280]{2,1,0:T(8,128)(2,1)}), bf16[32,8,1280]{2,1,0:T(8,128)(2,1)}, u32[]{:S(2)}, u32[]{:S(2)}) async-start(bf16[32,8,1280]{2,1,0:T(8,128)(2,1)} %divide_convert_fusion), calls=%async_computation | async-start | bytes 1310720 | tf_op jit(solution)/shard_map/all_to_all | solution.py:28
  155.2 93.9 %all-reduce.5.cloned.1.call-start = ((), (), s32[]{:S(2)}) async-start(), calls=%async_computation.3 | async-start | bytes 2621440 | tf_op jit(solution)/shard_map/psum | solution.py:39
  181.3 0.7 copy-start.2
  249.1 27.3 %copy-start.1 = (f32[1152,256]{0,1:T(8,128)S(1)}, f32[1152,256]{0,1:T(8,128)}, u32[]{:S(2)}) copy-start(f32[1152,256]{0,1:T(8,128)} %get-tuple-element.9) | copy-start | bytes 3538948
Sparse Core Ops, SparseCore 0:
  81.6 61.5 all-reduce.2
  181.5 67.5 all-reduce.4
where the time goes:
time: 290 us; the launch traced here: 286 us
  waiting for transfers between devices  123 us (42%)
  blocking collectives  113 us (39%)
  matrix products  15.4 us (5%)
  between operations  13.4 us (5%)
  starting transfers between devices  9.7 us (3%)
  local copies, waits for them, and re-layouts  5.99 us (2%)
  other arithmetic  5.47 us (2%)
    psum x1, waiting for transfers between devices, on_device(): expert_sum = lax.psum(partial_out, 'narrow')  67 us
    all_gather x1, blocking collectives, on_device(): lax.all_gather(slot_keys, 'wide', axis=1, tiled=True)  42.5 us
    psum x1, waiting for transfers between devices, on_device(): summed, summed_totals = lax.psum((slot_sums, totals), 'narrow')  39.5 us
    all_to_all x1, blocking collectives, on_device(): lax.all_to_all(slot_outputs, 'wide', split_axis=0, concat_axis=0, tiled=T...  25.8 us
    pmax x1, blocking collectives, on_device(): column_top = lax.pmax(jnp.max(logits, axis=0), 'narrow')  24.1 us
    psum x1, blocking collectives, on_device(): summed, summed_totals = lax.psum((slot_sums, totals), 'narrow')  20.5 us
    all_to_all x1, waiting for transfers between devices, on_device(): lax.all_to_all(slot_inputs, 'wide', split_axis=0, concat_axis=0, tiled=True)  16.4 us
    all_to_all x1, starting transfers between devices, on_device(): lax.all_to_all(slot_inputs, 'wide', split_axis=0, concat_axis=0, tiled=True)  9.65 us
  transfers between devices with their start and end apart: 3, of which 3 were waited for; matrix products, arithmetic and copies ran while one was open for 1% of the time, Pallas kernels for 0%

commit v1 on v0

v1 whole, which is shorter than its diff:
```python
import jax
import jax.numpy as jnp
from jax import lax
from jax.experimental import pallas as pl
from jax.experimental.pallas import tpu as pltpu
from jax.sharding import PartitionSpec as P

MESH = pl.DeviceIdType.MESH
BF = jnp.bfloat16
F32 = jnp.float32
NZ, NX, NY = 8, 4, 4
OWN = 8
D = 1280


def kernel(
    tok_hbm, key_hbm, win_hbm, bin_ref, wout_hbm, bout_ref,
    comb_ref, back_ref,
    tok, win, wout, own_key, keys, lt, comb,
    sums, stat, sib_sums, sib_stat, half, half_stat, far, far_stat,
    ready, slots_in, part, sib_part, half2, far2, ready2, back,
    load_sem, key_send, key_recv, fwd_send, fwd_recv,
    a_send, a_recv, b_send, b_recv, c_send, c_recv, d_send, d_recv, e_send, e_recv,
    f_send, f_recv, g_send, g_recv, i_send, i_recv, j_send, j_recv, k_send, k_recv,
):
    w, n = lax.axis_index("wide"), lax.axis_index("narrow")
    z, x = w // NX, lax.rem(w, NX)
    y, c = n // 2, lax.rem(n, 2)
    sib = (w, y * 2 + 1 - c)
    h = lax.rem(z // 4 + c, 2)
    gx = lax.rem(y + NX - x, NX)

    def y_peer(k):
        return (w, lax.rem(y + k, NY) * 2 + c)

    def send(src, dst, s_sem, r_sem, dev):
        cp = pltpu.make_async_remote_copy(
            src_ref=src, dst_ref=dst, send_sem=s_sem, recv_sem=r_sem, device_id=dev, device_id_type=MESH
        )
        cp.start()
        return cp

    def wait_for(ref, sem):
        pltpu.make_async_copy(ref, ref, sem).wait()

    loads = [
        pltpu.make_async_copy(key_hbm, own_key, load_sem.at[0]),
        pltpu.make_async_copy(tok_hbm, tok, load_sem.at[1]),
        pltpu.make_async_copy(win_hbm, win, load_sem.at[2]),
        pltpu.make_async_copy(wout_hbm, wout, load_sem.at[3]),
    ]
    for cp in loads:
        cp.start()

    barrier = pltpu.get_barrier_semaphore()

    def greet(w_to, n_to):
        pl.semaphore_signal(barrier, inc=1, device_id=(w_to, n_to), device_id_type=MESH)

    greet(*sib)
    for k in range(1, NY):
        greet(*y_peer(k))
    order = (4, 3, 5, 2, 6, 1, 7, 0)

    def key_peer(di, dz):
        return (lax.rem(z + dz, NZ) * NX + lax.rem(x + c + 2 * di, NX), n)

    for dz in order:
        for di in (1, 0):
            if di == 0 and dz == 0:
                @pl.when(c == 1)
                def _():
                    greet(*key_peer(0, 0))
            else:
                greet(*key_peer(di, dz))
    pl.semaphore_wait(barrier, 1 + (NY - 1) + 2 * NZ - 1 + c)
    loads[0].wait()

    own_copy = pltpu.make_async_copy(own_key, keys.at[x, z], key_recv.at[0])
    key_copies = []
    for i, dz in enumerate(order):
        for di in (1, 0):
            cp = pltpu.make_async_remote_copy(
                src_ref=own_key, dst_ref=keys.at[x, z], send_sem=key_send.at[di * NZ + dz],
                recv_sem=key_recv.at[di], device_id=key_peer(di, dz), device_id_type=MESH,
            )
            if di == 0 and dz == 0:
                @pl.when(c == 1)
                def _():
                    cp.start()
                @pl.when(c == 0)
                def _():
                    own_copy.start()
            else:
                cp.start()
            key_copies.append((di, dz, cp))
    fwd = []
    for di in (0, 1):
        xs = lax.rem(x + NX - c - 2 * di + NX, NX)
        wait_for(keys.at[xs], key_recv.at[di])
        fwd.append(send(keys.at[xs], keys.at[xs], fwd_send.at[di], fwd_recv.at[di], sib))
    for di in (0, 1):
        xs = lax.rem(x + NX - (1 - c) - 2 * di + NX, NX)
        wait_for(keys.at[xs], fwd_recv.at[di])
    loads[1].wait()

    key_rows = keys[...].reshape(NX * NZ * OWN, D)
    tokens = tok.shape[0]
    step = tokens // 3
    for i in range(3):
        lt[:, i * step:(i + 1) * step] = lax.dot_general(
            key_rows, tok[i * step:(i + 1) * step, :], (((1,), (1,)), ((), ())), preferred_element_type=F32
        )
    logits_t = lt[...]
    top = jnp.max(logits_t, axis=1, keepdims=True)
    spread = jnp.exp(logits_t - top)
    totals = jnp.sum(spread, axis=1, keepdims=True)
    dispatch = spread.astype(BF)
    slots = dispatch.shape[0]
    lane = lax.broadcasted_iota(jnp.int32, (slots, 128), 1)
    stat[...] = jnp.where(lane < 64, top, totals).reshape(stat.shape)
    for i in range(5):
        cols = slice(i * 256, (i + 1) * 256)
        sums[:, :, :, cols] = (
            jnp.dot(dispatch, tok[:, cols], preferred_element_type=F32).astype(BF).reshape(NX, 2, 32, 256)
        )

    a = [
        send(sums.at[:, 1 - h], sib_sums, a_send.at[0], a_recv.at[0], sib),
        send(stat.at[:, 1 - h], sib_stat, a_send.at[1], a_recv.at[1], sib),
    ]

    for i in range(4):
        rows = slice(i * (tokens // 4), (i + 1) * (tokens // 4))
        logits = lax.dot_general(
            tok[rows, :], key_rows, (((1,), (1,)), ((), ())), preferred_element_type=F32
        )
        row_spread = jnp.exp(logits - jnp.max(logits, axis=1, keepdims=True))
        comb[rows, :] = (row_spread / jnp.sum(row_spread, axis=1, keepdims=True)).astype(BF)
    comb_out = pltpu.make_async_copy(comb, comb_ref, load_sem.at[4])
    comb_out.start()

    for cp in a:
        cp.wait_recv()
    lane = lax.broadcasted_iota(jnp.int32, (32, 128), 1)
    for j in range(NX):
        st_a, st_b = stat[j, h], sib_stat[j]
        m_a, t_a, m_b, t_b = st_a[:, 0:1], st_a[:, 64:65], st_b[:, 0:1], st_b[:, 64:65]
        m = jnp.maximum(m_a, m_b)
        f_a, f_b = jnp.exp(m_a - m), jnp.exp(m_b - m)
        half[j] = (sums[j, h].astype(F32) * f_a + sib_sums[j].astype(F32) * f_b).astype(BF)
        half_stat[j] = jnp.where(lane < 64, m, t_a * f_a + t_b * f_b)

    b = []
    for k in (2, 1, 3):
        to = lax.rem(y + k + NX - x, NX)
        b.append(send(half.at[to], far.at[k - 1], b_send.at[k - 1], b_recv.at[k - 1], y_peer(k)))
        b.append(send(half_stat.at[to], far_stat.at[k - 1], b_send.at[k + 2], b_recv.at[k + 2], y_peer(k)))
    for cp in b:
        cp.wait_recv()
    st = [half_stat[gx]] + [far_stat[k] for k in range(3)]
    ms = [s[:, 0:1] for s in st]
    ts = [s[:, 64:65] for s in st]
    m = jnp.maximum(jnp.maximum(ms[0], ms[1]), jnp.maximum(ms[2], ms[3]))
    fs = [jnp.exp(mi - m) for mi in ms]
    inv = 1.0 / (ts[0] * fs[0] + ts[1] * fs[1] + ts[2] * fs[2] + ts[3] * fs[3])
    acc = half[gx].astype(F32) * (fs[0] * inv)
    for k in range(3):
        acc = acc + far[k].astype(F32) * (fs[k + 1] * inv)
    ready[...] = acc.reshape(4, OWN, D).astype(BF)

    def plane(src, there, here, s_sem, r_sem):
        copies = []
        for i in range(4):
            w_to = (4 * h + i) * NX + gx
            cp = pltpu.make_async_remote_copy(
                src_ref=src.at[i], dst_ref=there, send_sem=s_sem.at[i], recv_sem=r_sem,
                device_id=(w_to, n), device_id_type=MESH,
            )

            @pl.when(w_to != w)
            def _():
                cp.start()

            @pl.when(w_to == w)
            def _():
                pltpu.make_async_copy(src.at[i], there, r_sem).start()

            copies.append((w_to, cp))
        wait_for(here, r_sem)
        return copies

    def gather(place, y_send, y_recv, s_send, s_recv):
        own = place(y, c)
        copies = [send(own, own, y_send.at[k - 1], y_recv.at[k - 1], y_peer(k)) for k in (2, 1, 3)]
        copies.append(send(own, own, s_send.at[0], s_recv.at[0], sib))
        for k in (1, 3, 2):
            got = place(lax.rem(y + NY - k, NY), c)
            wait_for(got, y_recv.at[k - 1])
            copies.append(send(got, got, s_send.at[k], s_recv.at[k], sib))
        for k in range(NY):
            wait_for(place(lax.rem(y + NY - k, NY), 1 - c), s_recv.at[k])
        return copies

    p1 = plane(ready, slots_in.at[n, lax.rem(z, 4)], slots_in.at[n], c_send, c_recv)
    g1 = gather(lambda yy, cc: slots_in.at[yy * 2 + cc], d_send, d_recv, e_send, e_recv)

    loads[2].wait()
    loads[3].wait()
    rows_in = slots_in[...].reshape(slots, D)
    first = lax.rem(lax.broadcasted_iota(jnp.int32, (slots, 1), 0), OWN) < 4
    b_in = bin_ref[...].astype(F32)
    hid = jnp.where(
        first,
        jnp.dot(rows_in, win[0], preferred_element_type=F32) + b_in[0:1],
        jnp.dot(rows_in, win[1], preferred_element_type=F32) + b_in[1:2],
    )
    hid = jax.nn.gelu(hid, approximate=True)
    hid0 = jnp.where(first, hid, 0.0).astype(BF)
    hid1 = jnp.where(first, 0.0, hid).astype(BF)
    for i in range(5):
        cols = slice(i * 256, (i + 1) * 256)
        out = jnp.dot(hid0, wout[0, :, cols], preferred_element_type=F32)
        out = out + jnp.dot(hid1, wout[1, :, cols], preferred_element_type=F32)
        part[:, :, :, cols] = out.astype(BF).reshape(NY, 2, 32, 256)

    f = send(part.at[:, 1 - c], sib_part, f_send, f_recv, sib)
    f.wait_recv()
    for j in range(NY):
        half2[j] = (part[j, c].astype(F32) + sib_part[j].astype(F32)).astype(BF)
    gs = [send(half2.at[lax.rem(y + k, NY)], far2.at[k - 1], g_send.at[k - 1], g_recv.at[k - 1], y_peer(k)) for k in (2, 1, 3)]
    for cp in gs:
        cp.wait_recv()
    b_out = bout_ref[...].astype(F32)
    first32 = lax.rem(lax.broadcasted_iota(jnp.int32, (32, 1), 0), OWN) < 4
    acc = half2[y].astype(F32) + jnp.where(first32, b_out[0:1], b_out[1:2])
    for k in range(3):
        acc = acc + far2[k].astype(F32)
    ready2[...] = acc.reshape(4, OWN, D).astype(BF)

    p2 = plane(ready2, back.at[x, z // 4, lax.rem(z, 4)], back.at[gx, h], i_send, i_recv)
    g2 = gather(
        lambda yy, cc: back.at[lax.rem(yy + NX - x, NX), lax.rem(z // 4 + cc, 2)], j_send, j_recv, k_send, k_recv
    )
    out_copy = pltpu.make_async_copy(back, back_ref, load_sem.at[5])
    out_copy.start()

    for di, dz, cp in key_copies:
        if di == 0 and dz == 0:
            @pl.when(c == 1)
            def _():
                cp.wait_send()
        else:
            cp.wait_send()
    for cp in fwd + a + b + g1 + [f] + gs + g2:
        cp.wait_send()
    for w_to, cp in p1 + p2:
        @pl.when(w_to != w)
        def _():
            cp.wait_send()
    comb_out.wait()
    out_copy.wait()


def on_device(tokens, slot_keys, w_in, b_in, w_out, b_out):
    rows = tokens.shape[1]
    slots = NZ * NX * OWN
    hbm = pl.BlockSpec(memory_space=pl.ANY)
    vmem = pl.BlockSpec(memory_space=pltpu.VMEM)
    dma = pltpu.SemaphoreType.DMA
    block = (4, OWN, D)
    comb, back = pl.pallas_call(
        kernel,
        out_shape=(
            jax.ShapeDtypeStruct((rows, slots), BF),
            jax.ShapeDtypeStruct((NX, 2) + block, BF),
        ),
        in_specs=[hbm, hbm, hbm, vmem, hbm, vmem],
        out_specs=(hbm, hbm),
        scratch_shapes=[
            pltpu.VMEM((rows, D), BF),
            pltpu.VMEM(w_in.shape, BF),
            pltpu.VMEM(w_out.shape, BF),
            pltpu.VMEM((OWN, D), BF),
            pltpu.VMEM((NX, NZ, OWN, D), BF),
            pltpu.VMEM((slots, rows), F32),
            pltpu.VMEM((rows, slots), BF),
            pltpu.VMEM((NX, 2, 32, D), BF),
            pltpu.VMEM((NX, 2, 32, 128), F32),
            pltpu.VMEM((NX, 32, D), BF),
            pltpu.VMEM((NX, 32, 128), F32),
            pltpu.VMEM((NX, 32, D), BF),
            pltpu.VMEM((NX, 32, 128), F32),
            pltpu.VMEM((3, 32, D), BF),
            pltpu.VMEM((3, 32, 128), F32),
            pltpu.VMEM(block, BF),
            pltpu.VMEM((8,) + block, BF),
            pltpu.VMEM((NY, 2, 32, D), BF),
            pltpu.VMEM((NY, 32, D), BF),
            pltpu.VMEM((NY, 32, D), BF),
            pltpu.VMEM((3, 32, D), BF),
            pltpu.VMEM(block, BF),
            pltpu.VMEM((NX, 2) + block, BF),
            dma((6,)), dma((16,)), dma((2,)), dma((2,)), dma((2,)),
            dma((2,)), dma((2,)), dma((6,)), dma((6,)), dma((4,)), dma, dma((3,)), dma((3,)), dma((4,)), dma((4,)),
            dma, dma, dma((3,)), dma((3,)), dma((4,)), dma, dma((3,)), dma((3,)), dma((4,)), dma((4,)),
        ],
        compiler_params=pltpu.CompilerParams(
            collective_id=0, has_side_effects=True, vmem_limit_bytes=48 * 1024 * 1024
        ),
    )(tokens[0], slot_keys.T, w_in, b_in, w_out, b_out)
    mixed = jnp.dot(comb, back.reshape(slots, D), preferred_element_type=F32)
    return mixed.astype(BF)[None]


def solution(mesh):
    in_specs = (
        P("wide", "narrow", None),
        P(None, "wide"),
        P("wide", None, "narrow"),
        P("wide", "narrow"),
        P("wide", "narrow", None),
        P("wide", None),
    )
    return jax.shard_map(
        on_device, mesh=mesh, in_specs=in_specs, out_specs=P("wide", "narrow", None), check_vma=False
    )
```

time: 290 us -> 74.1 us (0.26); the launches traced: 286 us -> 73.8 us
  waiting for transfers between devices: 123 us -> 0 us
  blocking collectives: 113 us -> 0 us
  Pallas kernels: 0 us -> 67.4 us
  between operations: 13.4 us -> 0.01 us
  matrix products: 15.4 us -> 2.53 us
  starting transfers between devices: 9.7 us -> 0 us
  other arithmetic: 5.47 us -> 0 us
    psum x2 -> x0, waiting for transfers between devices: 107 us -> none  [the longest x1 67 us: on_device(): expert_sum = lax.psum(partial_out, 'narrow')]
    pallas_call x0 -> x1, Pallas kernels: none -> 67.4 us  [on_device(): pl.pallas_call(kernel, out_shape=(jax.ShapeDtypeStruct((rows, slots), BF)...]
    all_gather x1 -> x0, blocking collectives: 42.5 us -> none  [on_device(): lax.all_gather(slot_keys, 'wide', axis=1, tiled=True)]
    all_to_all x1 -> x0, blocking collectives: 25.8 us -> none  [on_device(): lax.all_to_all(slot_outputs, 'wide', split_axis=0, concat_axis=0, tiled=T...]
    pmax x1 -> x0, blocking collectives: 24.1 us -> none  [on_device(): column_top = lax.pmax(jnp.max(logits, axis=0), 'narrow')]
    psum x1 -> x0, blocking collectives: 20.5 us -> none  [on_device(): summed, summed_totals = lax.psum((slot_sums, totals), 'narrow')]
    all_to_all x1 -> x0, waiting for transfers between devices: 16.4 us -> none  [on_device(): lax.all_to_all(slot_inputs, 'wide', split_axis=0, concat_axis=0, tiled=True)]
    dot_general x4 -> x1, matrix products: 15.4 us -> 2.53 us  [on_device(): mixed = jnp.dot(comb, back.reshape(slots, D), preferred_element_type=F32)]
  transfers between devices with their start and end apart: 3 -> 0, of which waited for: 3 -> 0; matrix products, arithmetic and copies ran while one was open for 1% -> 0% of each run, Pallas kernels for 0% -> 0%
where the time goes in v1:
time: 74.1 us; the launch traced here: 73.8 us
  Pallas kernels  67.4 us (91%)
  local copies, waits for them, and re-layouts  3.93 us (5%)
  matrix products  2.53 us (3%)
    pallas_call x1, Pallas kernels, on_device(): pl.pallas_call(kernel, out_shape=(jax.ShapeDtypeStruct((rows, slots), BF)...  67.4 us
    unnamed x8, local copies, waits for them, and re-layouts  3.93 us
    dot_general x1, matrix products, on_device(): mixed = jnp.dot(comb, back.reshape(slots, D), preferred_element_type=F32)  2.53 us

profile of v1, /device:TPU:1, one launch (start us, length us, event | category | flops | bytes accessed | tf_op | source)
XLA Modules:
  0.0 73.8 jit_solution(7331513534438169091)
XLA Ops:
  0.0 0.0 copy-start
  0.0 1.8 %copy-done = bf16[1,1152,1280]{2,1,0:T(8,128)(2,1)S(1)} copy-done((bf16[1,1152,1280]{2,1,0:T(8,128)(2,1)S(1)}, bf16[1,1152,1280]{2,1,0:T(8,128)(2,1)}, u32[]{:S(2)}) %copy-start) | copy-done | bytes 2949144
  1.8 0.0 copy-start.1
  1.8 0.7 copy-done.1
  2.6 0.0 copy-start.2
  2.6 0.7 copy-done.2
  3.3 0.0 copy-start.3
  3.3 0.7 copy-done.3
  3.9 67.4 %shard_map.64 = (bf16[1152,256]{1,0:T(8,128)(2,1)S(1)}, bf16[4,2,4,8,1280]{4,3,2,1,0:T(8,128)(2,1)S(1)}) custom-call(bf16[1152,1280]{1,0:T(8,128)(2,1)S(1)} %bitcast.7, bf16[8,1280]{1,0:T(8,128)(2,1)S(1)} %bitcast.8, bf16[2,1280,640]{2,1,0:T(8,128)(2,1)} %win_hbm.1, bf16[2,640]{1,0:T(2,128)(2,1)S(1)} %copy-done.3, bf16[2,640,1280]{2,1,0:T(8,128)(2,1)} %wout_hbm.1, ...), custom_call_target="tpu_custom_call" | custom-call | tf_op jit(solution)/shard_map/pallas_call | solution.py:272
  71.3 2.5 %fusion = bf16[1,1152,1280]{2,1,0:T(8,128)(2,1)} fusion(bf16[1152,256]{1,0:T(8,128)(2,1)S(1)} %get-tuple-element.7, bf16[256,1280]{1,0:T(8,128)(2,1)S(1)} %bitcast.9), kind=kOutput, calls=%fused_computation.1 | convolution fusion | flops 756449280 | bytes 4194304 | tf_op jit(solution)/shard_map/dot_general | solution.py:312
Async XLA Ops:
  0.0 1.8 %copy-start = (bf16[1,1152,1280]{2,1,0:T(8,128)(2,1)S(1)}, bf16[1,1152,1280]{2,1,0:T(8,128)(2,1)}, u32[]{:S(2)}) copy-start(bf16[1,1152,1280]{2,1,0:T(8,128)(2,1)} %param.6) | copy-start | bytes 8847364
  1.8 0.7 copy-start.1
  2.6 0.7 copy-start.2
  3.3 0.7 copy-start.3

commit v2 on v0

v2 whole, which is shorter than its diff:
```python
import jax
import jax.numpy as jnp
from jax import lax
from jax.experimental import pallas as pl
from jax.experimental.pallas import tpu as pltpu
from jax.sharding import PartitionSpec as P

MESH = pl.DeviceIdType.MESH
BF = jnp.bfloat16
F32 = jnp.float32
NZ, NX, NY = 8, 4, 4
OWN = 8
D = 1280
PARTS = ((0, 768), (768, 512))
Q = len(PARTS)


def kernel(
    tok_hbm, key_hbm, win_hbm, bin_hbm, wout_hbm, bout_hbm,
    comb_ref, back,
    tok, win, wout, b_in, b_out, own_key, keys, lt, comb,
    sums, stat, sib_sums, sib_stat, own_sums, half, half_stat, far, far_stat,
    ready, slots_in, part, own_part, sib_part, half2, own2, far2, ready2,
    load_sem, key_send, key_recv, fwd_send, fwd_recv,
    as_send, as_recv, a_send, a_recv, bs_send, bs_recv, b_send, b_recv,
    c_send, c_recv, d_send, d_recv, e_send, e_recv,
    f_send, f_recv, g_send, g_recv, i_send, i_recv, j_send, j_recv, k_send, k_recv,
):
    w, n = lax.axis_index("wide"), lax.axis_index("narrow")
    z, x = w // NX, lax.rem(w, NX)
    y, c = n // 2, lax.rem(n, 2)
    sib = (w, y * 2 + 1 - c)
    h = lax.rem(z // 4 + c, 2)
    q_half = 1 - h
    gx = lax.rem(y + NX - x, NX)
    tokens = tok.shape[0]
    started = []

    def y_peer(k):
        return (w, lax.rem(y + k, NY) * 2 + c)

    def cols(q):
        return pl.ds(*PARTS[q])

    def remote(src, dst, s_sem, r_sem, dev):
        return pltpu.make_async_remote_copy(
            src_ref=src, dst_ref=dst, send_sem=s_sem, recv_sem=r_sem, device_id=dev, device_id_type=MESH
        )

    def send(src, dst, s_sem, r_sem, dev):
        cp = remote(src, dst, s_sem, r_sem, dev)
        cp.start()
        started.append((None, cp))

    def send_wide(src, dst, s_sem, r_sem, w_to):
        cp = remote(src, dst, s_sem, r_sem, (w_to, n))

        @pl.when(w_to != w)
        def _():
            cp.start()

        @pl.when(w_to == w)
        def _():
            pltpu.make_async_copy(src, dst, r_sem).start()

        started.append((w_to, cp))

    def drain():
        for w_to, cp in started:
            if w_to is None:
                cp.wait_send()
            else:
                @pl.when(w_to != w)
                def _():
                    cp.wait_send()
        started.clear()

    def wait_for(ref, sem):
        pltpu.make_async_copy(ref, ref, sem).wait()

    loads = [
        pltpu.make_async_copy(src, dst, load_sem.at[i])
        for i, (src, dst) in enumerate((
            (key_hbm, own_key), (tok_hbm, tok),
            (win_hbm.at[0], win.at[:, pl.ds(0, 640)]), (win_hbm.at[1], win.at[:, pl.ds(640, 640)]),
            (wout_hbm, wout), (bin_hbm, b_in), (bout_hbm, b_out),
        ))
    ]
    for cp in loads:
        cp.start()

    barrier = pltpu.get_barrier_semaphore()

    def greet(w_to, n_to):
        pl.semaphore_signal(barrier, inc=1, device_id=(w_to, n_to), device_id_type=MESH)

    key_peers = [(dx, (4 * q_half + i) * NX + lax.rem(x + dx, NX)) for dx in (2, 1, 3, 0) for i in range(4)]
    for dx, w_to in key_peers:
        if dx:
            greet(w_to, n)
        else:
            @pl.when(w_to != w)
            def _():
                greet(w_to, n)
    for k in (2, 1, 3):
        greet(*y_peer(k))
    greet(*sib)
    pl.semaphore_wait(barrier, 20 - c)
    loads[0].wait()

    for p, (dx, w_to) in enumerate(key_peers):
        dst = keys.at[x, z // 4, lax.rem(z, 4)]
        if dx:
            send(own_key, dst, key_send.at[p], key_recv.at[dx], (w_to, n))
        else:
            send_wide(own_key, dst, key_send.at[p], key_recv.at[dx], w_to)
    loads[1].wait()
    for dx in (0, 1, 3, 2):
        got = keys.at[lax.rem(x + NX - dx, NX), q_half]
        wait_for(got, key_recv.at[dx])
        send(got, got, fwd_send.at[dx], fwd_recv.at[dx], sib)

    def column_softmax(half_index):
        key_rows = keys[:, half_index].reshape(128, D)
        step = tokens // 3
        for i in range(3):
            lt[:, i * step:(i + 1) * step] = lax.dot_general(
                key_rows, tok[i * step:(i + 1) * step, :], (((1,), (1,)), ((), ())), preferred_element_type=F32
            )
        logits = lt[...]
        top = jnp.max(logits, axis=1, keepdims=True)
        spread = jnp.exp(logits - top)
        return top, jnp.sum(spread, axis=1, keepdims=True), spread.astype(BF)

    lane = lax.broadcasted_iota(jnp.int32, (128, 128), 1)
    top, totals, dispatch = column_softmax(q_half)
    stat[...] = jnp.where(lane < 64, top, totals).reshape(NX, 32, 128)
    send(stat, sib_stat, as_send, as_recv, sib)
    for q, (at, size) in enumerate(PARTS):
        sums[:, :, cols(q)] = (
            jnp.dot(dispatch, tok[:, cols(q)], preferred_element_type=F32).astype(BF).reshape(NX, 32, size)
        )
        send(sums.at[:, :, cols(q)], sib_sums.at[:, :, cols(q)], a_send.at[q], a_recv.at[q], sib)
    for dx in (0, 1, 3, 2):
        wait_for(keys.at[lax.rem(x + NX - dx, NX), h], fwd_recv.at[dx])
    top, totals, dispatch = column_softmax(h)
    wait_for(sib_stat, as_recv)
    other = sib_stat[...].reshape(128, 128)
    other_top, other_totals = other[:, 0:1], other[:, 64:65]
    chip_top = jnp.maximum(top, other_top)
    own_scale, other_scale = jnp.exp(top - chip_top), jnp.exp(other_top - chip_top)
    chip_totals = totals * own_scale + other_totals * other_scale
    half_stat[...] = jnp.where(lane < 64, chip_top, chip_totals).reshape(NX, 32, 128)
    for k in (2, 1, 3):
        to = lax.rem(y + k + NX - x, NX)
        send(half_stat.at[to], far_stat.at[k - 1], bs_send.at[k - 1], bs_recv.at[k - 1], y_peer(k))
    for q, (at, size) in enumerate(PARTS):
        mine = jnp.dot(dispatch, tok[:, cols(q)], preferred_element_type=F32) * own_scale
        wait_for(sib_sums.at[:, :, cols(q)], a_recv.at[q])
        chip = mine + sib_sums[:, :, cols(q)].astype(F32).reshape(128, size) * other_scale
        own_sums[:, :, cols(q)] = chip.reshape(NX, 32, size)
        half[:, :, cols(q)] = chip.astype(BF).reshape(NX, 32, size)
        for k in (2, 1, 3):
            to = lax.rem(y + k + NX - x, NX)
            send(half.at[to, :, cols(q)], far.at[k - 1, :, cols(q)], b_send.at[q, k - 1], b_recv.at[q, k - 1], y_peer(k))

    key_rows = keys[...].reshape(256, D)
    for i in range(4):
        rows = slice(i * (tokens // 4), (i + 1) * (tokens // 4))
        logits = lax.dot_general(
            tok[rows, :], key_rows, (((1,), (1,)), ((), ())), preferred_element_type=F32
        )
        row_spread = jnp.exp(logits - jnp.max(logits, axis=1, keepdims=True))
        comb[rows, :] = (row_spread / jnp.sum(row_spread, axis=1, keepdims=True)).astype(BF)
    comb_out = pltpu.make_async_copy(comb, comb_ref, load_sem.at[7])
    comb_out.start()

    for k in (1, 3, 2):
        wait_for(far_stat.at[k - 1], bs_recv.at[k - 1])
    st = [half_stat[gx]] + [far_stat[k] for k in range(3)]
    ms = [s[:, 0:1] for s in st]
    ts = [s[:, 64:65] for s in st]
    m = jnp.maximum(jnp.maximum(ms[0], ms[1]), jnp.maximum(ms[2], ms[3]))
    fs = [jnp.exp(mi - m) for mi in ms]
    inv = 1.0 / (ts[0] * fs[0] + ts[1] * fs[1] + ts[2] * fs[2] + ts[3] * fs[3])
    fs = [f * inv for f in fs]

    def plane(src, there, s_sem, r_sem):
        for i in range(4):
            send_wide(src(i), there, s_sem.at[i], r_sem, (4 * h + i) * NX + gx)

    def gather_start(place, y_send, y_recv, s_send, s_recv):
        own = place(y, c)
        for k in (2, 1, 3):
            send(own, own, y_send.at[k - 1], y_recv.at[k - 1], y_peer(k))
        send(own, own, s_send.at[0], s_recv.at[0], sib)

    def gather_forward(place, y_send, y_recv, s_send, s_recv):
        for k in (1, 3, 2):
            got = place(lax.rem(y + NY - k, NY), c)
            wait_for(got, y_recv.at[k - 1])
            send(got, got, s_send.at[k], s_recv.at[k], sib)

    def gather_end(place, y_send, y_recv, s_send, s_recv):
        for k in range(NY):
            wait_for(place(lax.rem(y + NY - k, NY), 1 - c), s_recv.at[k])

    for q, (at, size) in enumerate(PARTS):
        for k in (1, 3, 2):
            wait_for(far.at[k - 1, :, cols(q)], b_recv.at[q, k - 1])
        acc = own_sums[gx, :, cols(q)] * fs[0]
        for k in range(3):
            acc = acc + far[k, :, cols(q)].astype(F32) * fs[k + 1]
        ready[:, :, cols(q)] = acc.reshape(4, OWN, size).astype(BF)
        plane(
            lambda i: ready.at[i, :, cols(q)], slots_in.at[n, lax.rem(z, 4), :, cols(q)], c_send.at[q], c_recv.at[q]
        )
    drain()

    def gather1(q):
        return (
            lambda yy, cc: slots_in.at[yy * 2 + cc, :, :, cols(q)], d_send.at[q], d_recv.at[q], e_send.at[q], e_recv.at[q]
        )

    for q in range(Q):
        wait_for(slots_in.at[n, :, :, cols(q)], c_recv.at[q])
        gather_start(*gather1(q))
    for q in range(Q):
        gather_forward(*gather1(q))

    for cp in loads[2:]:
        cp.wait()
    hid = None
    for q, (at, size) in enumerate(PARTS):
        gather_end(*gather1(q))
        rows_in = slots_in[:, :, :, cols(q)].reshape(256, size)
        term = jnp.dot(rows_in, win[cols(q), :], preferred_element_type=F32)
        hid = term if hid is None else hid + term
    first = lax.rem(lax.broadcasted_iota(jnp.int32, (256, 1), 0), OWN) < 4
    bias = b_in[...].astype(F32)
    hid = jnp.where(first, hid[:, :640] + bias[0:1], hid[:, 640:] + bias[1:2])
    hid = jax.nn.gelu(hid, approximate=True)
    hid = jnp.concatenate((jnp.where(first, hid, 0.0).astype(BF), jnp.where(first, 0.0, hid).astype(BF)), axis=1)
    for q, (at, size) in enumerate(PARTS):
        out = jnp.dot(hid, wout[:, cols(q)], preferred_element_type=F32)
        part[:, :, :, cols(q)] = out.astype(BF).reshape(NY, 2, 32, size)
        send(part.at[:, 1 - c, :, cols(q)], sib_part.at[:, :, cols(q)], f_send.at[q], f_recv.at[q], sib)
        own_part[:, :, :, cols(q)] = out.reshape(NY, 2, 32, size)

    for q, (at, size) in enumerate(PARTS):
        wait_for(sib_part.at[:, :, cols(q)], f_recv.at[q])
        for j in range(NY):
            chip = own_part[j, c, :, cols(q)] + sib_part[j, :, cols(q)].astype(F32)
            own2[j, :, cols(q)] = chip
            half2[j, :, cols(q)] = chip.astype(BF)
        for k in (2, 1, 3):
            send(
                half2.at[lax.rem(y + k, NY), :, cols(q)], far2.at[k - 1, :, cols(q)],
                g_send.at[q, k - 1], g_recv.at[q, k - 1], y_peer(k),
            )
    drain()
    bias = b_out[...].astype(F32)
    first = lax.rem(lax.broadcasted_iota(jnp.int32, (32, 1), 0), OWN) < 4
    bias = jnp.where(first, bias[0:1], bias[1:2])
    for q, (at, size) in enumerate(PARTS):
        for k in (1, 3, 2):
            wait_for(far2.at[k - 1, :, cols(q)], g_recv.at[q, k - 1])
        acc = own2[y, :, cols(q)] + bias[:, at:at + size]
        for k in range(3):
            acc = acc + far2[k, :, cols(q)].astype(F32)
        ready2[:, :, cols(q)] = acc.reshape(4, OWN, size).astype(BF)
        plane(
            lambda i: ready2.at[i, :, cols(q)], back.at[x, z // 4, lax.rem(z, 4), :, cols(q)], i_send.at[q], i_recv.at[q]
        )
    drain()

    def gather2(q):
        return (
            lambda yy, cc: back.at[lax.rem(yy + NX - x, NX), lax.rem(z // 4 + cc, 2), :, :, cols(q)],
            j_send.at[q], j_recv.at[q], k_send.at[q], k_recv.at[q],
        )

    for q in range(Q):
        wait_for(back.at[gx, h, :, :, cols(q)], i_recv.at[q])
        gather_start(*gather2(q))
    comb_out.wait()
    for q in range(Q):
        gather_forward(*gather2(q))
    for q in range(Q):
        gather_end(*gather2(q))
    drain()


def on_device(tokens, slot_keys, w_in, b_in, w_out, b_out):
    rows = tokens.shape[1]
    slots = NZ * NX * OWN
    hbm = pl.BlockSpec(memory_space=pltpu.HBM)
    anywhere = pl.BlockSpec(memory_space=pl.ANY)
    dma = pltpu.SemaphoreType.DMA
    block = (4, OWN, D)
    comb, back = pl.pallas_call(
        kernel,
        out_shape=(
            jax.ShapeDtypeStruct((rows, slots), BF),
            jax.ShapeDtypeStruct((NX, 2) + block, BF),
        ),
        in_specs=[hbm] * 6,
        out_specs=(anywhere, anywhere),
        scratch_shapes=[
            pltpu.VMEM((rows, D), BF),
            pltpu.VMEM((D, D), BF),
            pltpu.VMEM((D, D), BF),
            pltpu.VMEM((2, 640), BF),
            pltpu.VMEM((2, D), BF),
            pltpu.VMEM((OWN, D), BF),
            pltpu.VMEM((NX, 2) + block, BF),
            pltpu.VMEM((slots // 2, rows), F32),
            pltpu.VMEM((rows, slots), BF),
            pltpu.VMEM((NX, 32, D), BF),
            pltpu.VMEM((NX, 32, 128), F32),
            pltpu.VMEM((NX, 32, D), BF),
            pltpu.VMEM((NX, 32, 128), F32),
            pltpu.VMEM((NX, 32, D), F32),
            pltpu.VMEM((NX, 32, D), BF),
            pltpu.VMEM((NX, 32, 128), F32),
            pltpu.VMEM((3, 32, D), BF),
            pltpu.VMEM((3, 32, 128), F32),
            pltpu.VMEM(block, BF),
            pltpu.VMEM((8,) + block, BF),
            pltpu.VMEM((NY, 2, 32, D), BF),
            pltpu.VMEM((NY, 2, 32, D), F32),
            pltpu.VMEM((NY, 32, D), BF),
            pltpu.VMEM((NY, 32, D), BF),
            pltpu.VMEM((NY, 32, D), F32),
            pltpu.VMEM((3, 32, D), BF),
            pltpu.VMEM(block, BF),
            dma((8,)), dma((16,)), dma((4,)), dma((4,)), dma((4,)),
            dma, dma, dma((Q,)), dma((Q,)), dma((3,)), dma((3,)), dma((Q, 3)), dma((Q, 3)),
            dma((Q, 4)), dma((Q,)), dma((Q, 3)), dma((Q, 3)), dma((Q, 4)), dma((Q, 4)),
            dma((Q,)), dma((Q,)), dma((Q, 3)), dma((Q, 3)),
            dma((Q, 4)), dma((Q,)), dma((Q, 3)), dma((Q, 3)), dma((Q, 4)), dma((Q, 4)),
        ],
        compiler_params=pltpu.CompilerParams(
            collective_id=0, has_side_effects=True, vmem_limit_bytes=60 * 1024 * 1024
        ),
    )(tokens[0], slot_keys.T, w_in, b_in, w_out.reshape(-1, D), b_out)
    mixed = jnp.dot(comb, back.reshape(slots, D), preferred_element_type=F32)
    return mixed.astype(BF)[None]


def solution(mesh):
    in_specs = (
        P("wide", "narrow", None),
        P(None, "wide"),
        P("wide", None, "narrow"),
        P("wide", "narrow"),
        P("wide", "narrow", None),
        P("wide", None),
    )
    return jax.shard_map(
        on_device, mesh=mesh, in_specs=in_specs, out_specs=P("wide", "narrow", None), check_vma=False
    )
```

time: 290 us -> 67.1 us (0.23); the launches traced: 286 us -> 67 us
  waiting for transfers between devices: 123 us -> 0 us
  blocking collectives: 113 us -> 0 us
  Pallas kernels: 0 us -> 63.2 us
  between operations: 13.4 us -> 0.01 us
  matrix products: 15.4 us -> 3.8 us
  starting transfers between devices: 9.7 us -> 0 us
  local copies, waits for them, and re-layouts: 5.99 us -> 0 us
  other arithmetic: 5.47 us -> 0 us
    psum x2 -> x0, waiting for transfers between devices: 107 us -> none  [the longest x1 67 us: on_device(): expert_sum = lax.psum(partial_out, 'narrow')]
    pallas_call x0 -> x1, Pallas kernels: none -> 63.2 us  [on_device(): pl.pallas_call(kernel, out_shape=(jax.ShapeDtypeStruct((rows, slots), BF)...]
    all_gather x1 -> x0, blocking collectives: 42.5 us -> none  [on_device(): lax.all_gather(slot_keys, 'wide', axis=1, tiled=True)]
    all_to_all x1 -> x0, blocking collectives: 25.8 us -> none  [on_device(): lax.all_to_all(slot_outputs, 'wide', split_axis=0, concat_axis=0, tiled=T...]
    pmax x1 -> x0, blocking collectives: 24.1 us -> none  [on_device(): column_top = lax.pmax(jnp.max(logits, axis=0), 'narrow')]
    psum x1 -> x0, blocking collectives: 20.5 us -> none  [on_device(): summed, summed_totals = lax.psum((slot_sums, totals), 'narrow')]
    all_to_all x1 -> x0, waiting for transfers between devices: 16.4 us -> none  [on_device(): lax.all_to_all(slot_inputs, 'wide', split_axis=0, concat_axis=0, tiled=True)]
    dot_general x4 -> x1, matrix products: 15.4 us -> 3.8 us  [on_device(): mixed = jnp.dot(comb, back.reshape(slots, D), preferred_element_type=F32)]
  transfers between devices with their start and end apart: 3 -> 0, of which waited for: 3 -> 0; matrix products, arithmetic and copies ran while one was open for 1% -> 0% of each run, Pallas kernels for 0% -> 0%
where the time goes in v2:
time: 67.1 us; the launch traced here: 67 us
  Pallas kernels  63.2 us (94%)
  matrix products  3.8 us (6%)
    pallas_call x1, Pallas kernels, on_device(): pl.pallas_call(kernel, out_shape=(jax.ShapeDtypeStruct((rows, slots), BF)...  63.2 us
    dot_general x1, matrix products, on_device(): mixed = jnp.dot(comb, back.reshape(slots, D), preferred_element_type=F32)  3.8 us

profile of v2, /device:TPU:1, one launch (start us, length us, event | category | flops | bytes accessed | tf_op | source)
XLA Modules:
  0.0 67.0 jit_solution(11785433230891900247)
XLA Ops:
  0.0 63.2 %shard_map.64 = (bf16[1152,256]{1,0:T(8,128)(2,1)}, bf16[4,2,4,8,1280]{4,3,2,1,0:T(8,128)(2,1)}) custom-call(bf16[1152,1280]{1,0:T(8,128)(2,1)} %bitcast.9, bf16[8,1280]{1,0:T(8,128)(2,1)} %bitcast.10, bf16[2,1280,640]{2,1,0:T(8,128)(2,1)} %win_hbm.1, bf16[2,640]{1,0:T(2,128)(2,1)} %bin_hbm.1, bf16[1280,1280]{1,0:T(8,128)(2,1)} %bitcast.8, ...), custom_call_target="tpu_custom_call" | custom-call | tf_op jit(solution)/shard_map/pallas_call | solution.py:301
  63.2 3.8 %fusion = bf16[1,1152,1280]{2,1,0:T(8,128)(2,1)} fusion(bf16[1152,256]{1,0:T(8,128)(2,1)} %get-tuple-element.7, bf16[256,1280]{1,0:T(8,128)(2,1)} %bitcast.11), kind=kOutput, calls=%fused_computation.1 | convolution fusion | flops 756449280 | bytes 4194304 | tf_op jit(solution)/shard_map/dot_general | solution.py:347

commit v3 on v2

--- a/solution.py
+++ b/solution.py
@@ -11,16 +11,16 @@
 NZ, NX, NY = 8, 4, 4
 OWN = 8
 D = 1280
-PARTS = ((0, 768), (768, 512))
+PARTS = ((0, 640), (640, 640))
 Q = len(PARTS)
 
 
 def kernel(
     tok_hbm, key_hbm, win_hbm, bin_hbm, wout_hbm, bout_hbm,
     comb_ref, back,
-    tok, win, wout, b_in, b_out, own_key, keys, lt, comb,
+    tok, tok_t, win, wout, b_in, b_out, own_key, keys, lt, comb,
     sums, stat, sib_sums, sib_stat, own_sums, half, half_stat, far, far_stat,
-    ready, slots_in, part, own_part, sib_part, half2, own2, far2, ready2,
+    ready, slots_in, part, own_part, sib_part, half2, far2, ready2,
     load_sem, key_send, key_recv, fwd_send, fwd_recv,
     as_send, as_recv, a_send, a_recv, bs_send, bs_recv, b_send, b_recv,
     c_send, c_recv, d_send, d_recv, e_send, e_recv,
@@ -115,6 +115,9 @@
         else:
             send_wide(own_key, dst, key_send.at[p], key_recv.at[dx], w_to)
     loads[1].wait()
+    step = tokens // 9
+    for i in range(9):
+        tok_t[:, i * step:(i + 1) * step] = tok[i * step:(i + 1) * step, :].T
     for dx in (0, 1, 3, 2):
         got = keys.at[lax.rem(x + NX - dx, NX), q_half]
         wait_for(got, key_recv.at[dx])
@@ -122,11 +125,9 @@
 
     def column_softmax(half_index):
         key_rows = keys[:, half_index].reshape(128, D)
-        step = tokens // 3
-        for i in range(3):
-            lt[:, i * step:(i + 1) * step] = lax.dot_general(
-                key_rows, tok[i * step:(i + 1) * step, :], (((1,), (1,)), ((), ())), preferred_element_type=F32
-            )
+        for i in range(0, tokens, 256):
+            to = min(tokens, i + 256)
+            lt[:, i:to] = jnp.dot(key_rows, tok_t[:, i:to], preferred_element_type=F32)
         logits = lt[...]
         top = jnp.max(logits, axis=1, keepdims=True)
         spread = jnp.exp(logits - top)
@@ -213,46 +214,53 @@
             acc = acc + far[k, :, cols(q)].astype(F32) * fs[k + 1]
         ready[:, :, cols(q)] = acc.reshape(4, OWN, size).astype(BF)
         plane(
-            lambda i: ready.at[i, :, cols(q)], slots_in.at[n, lax.rem(z, 4), :, cols(q)], c_send.at[q], c_recv.at[q]
+            lambda i: ready.at[i, :, cols(q)], slots_in.at[y, c, lax.rem(z, 4), :, cols(q)], c_send.at[q], c_recv.at[q]
         )
     drain()
 
     def gather1(q):
         return (
-            lambda yy, cc: slots_in.at[yy * 2 + cc, :, :, cols(q)], d_send.at[q], d_recv.at[q], e_send.at[q], e_recv.at[q]
-        )
-
-    for q in range(Q):
-        wait_for(slots_in.at[n, :, :, cols(q)], c_recv.at[q])
+            lambda yy, cc: slots_in.at[yy, cc, :, :, cols(q)], d_send.at[q], d_recv.at[q], e_send.at[q], e_recv.at[q]
+        )
+
+    for q in range(Q):
+        wait_for(slots_in.at[y, c, :, :, cols(q)], c_recv.at[q])
         gather_start(*gather1(q))
     for q in range(Q):
         gather_forward(*gather1(q))
 
     for cp in loads[2:]:
         cp.wait()
-    hid = None
-    for q, (at, size) in enumerate(PARTS):
+    first = lax.rem(lax.broadcasted_iota(jnp.int32, (128, 1), 0), OWN) < 4
+    bias = b_in[...].astype(F32)
+
+    def hidden(core):
+        hid = None
+        for q, (at, size) in enumerate(PARTS):
+            rows_in = slots_in[:, core, :, :, cols(q)].reshape(128, size)
+            term = jnp.dot(rows_in, win[cols(q), :], preferred_element_type=F32)
+            hid = term if hid is None else hid + term
+        hid = jnp.where(first, hid[:, :640] + bias[0:1], hid[:, 640:] + bias[1:2])
+        hid = jax.nn.gelu(hid, approximate=True)
+        return jnp.concatenate((jnp.where(first, hid, 0.0).astype(BF), jnp.where(first, 0.0, hid).astype(BF)), axis=1)
+
+    hid_c = hidden(c)
+    for q in range(Q):
         gather_end(*gather1(q))
-        rows_in = slots_in[:, :, :, cols(q)].reshape(256, size)
-        term = jnp.dot(rows_in, win[cols(q), :], preferred_element_type=F32)
-        hid = term if hid is None else hid + term
-    first = lax.rem(lax.broadcasted_iota(jnp.int32, (256, 1), 0), OWN) < 4
-    bias = b_in[...].astype(F32)
-    hid = jnp.where(first, hid[:, :640] + bias[0:1], hid[:, 640:] + bias[1:2])
-    hid = jax.nn.gelu(hid, approximate=True)
-    hid = jnp.concatenate((jnp.where(first, hid, 0.0).astype(BF), jnp.where(first, 0.0, hid).astype(BF)), axis=1)
-    for q, (at, size) in enumerate(PARTS):
-        out = jnp.dot(hid, wout[:, cols(q)], preferred_element_type=F32)
-        part[:, :, :, cols(q)] = out.astype(BF).reshape(NY, 2, 32, size)
-        send(part.at[:, 1 - c, :, cols(q)], sib_part.at[:, :, cols(q)], f_send.at[q], f_recv.at[q], sib)
-        own_part[:, :, :, cols(q)] = out.reshape(NY, 2, 32, size)
+    hid_sib = hidden(1 - c)
+    for q, (at, size) in enumerate(PARTS):
+        out = jnp.dot(hid_sib, wout[:, cols(q)], preferred_element_type=F32)
+        part[:, :, cols(q)] = out.astype(BF).reshape(NY, 32, size)
+        send(part.at[:, :, cols(q)], sib_part.at[:, :, cols(q)], f_send.at[q], f_recv.at[q], sib)
+    for q, (at, size) in enumerate(PARTS):
+        out = jnp.dot(hid_c, wout[:, cols(q)], preferred_element_type=F32)
+        own_part[:, :, cols(q)] = out.reshape(NY, 32, size)
 
     for q, (at, size) in enumerate(PARTS):
         wait_for(sib_part.at[:, :, cols(q)], f_recv.at[q])
-        for j in range(NY):
-            chip = own_part[j, c, :, cols(q)] + sib_part[j, :, cols(q)].astype(F32)
-            own2[j, :, cols(q)] = chip
-            half2[j, :, cols(q)] = chip.astype(BF)
+        chip = own_part[:, :, cols(q)] + sib_part[:, :, cols(q)].astype(F32)
+        own_part[:, :, cols(q)] = chip
+        half2[:, :, cols(q)] = chip.astype(BF)
         for k in (2, 1, 3):
             send(
                 half2.at[lax.rem(y + k, NY), :, cols(q)], far2.at[k - 1, :, cols(q)],
@@ -265,7 +273,7 @@
     for q, (at, size) in enumerate(PARTS):
         for k in (1, 3, 2):
             wait_for(far2.at[k - 1, :, cols(q)], g_recv.at[q, k - 1])
-        acc = own2[y, :, cols(q)] + bias[:, at:at + size]
+        acc = own_part[y, :, cols(q)] + bias[:, at:at + size]
         for k in range(3):
             acc = acc + far2[k, :, cols(q)].astype(F32)
         ready2[:, :, cols(q)] = acc.reshape(4, OWN, size).astype(BF)
@@ -301,13 +309,14 @@
     comb, back = pl.pallas_call(
         kernel,
         out_shape=(
-            jax.ShapeDtypeStruct((rows, slots), BF),
-            jax.ShapeDtypeStruct((NX, 2) + block, BF),
+            pltpu.VMEM((rows, slots), BF),
+            pltpu.VMEM((NX, 2) + block, BF),
         ),
         in_specs=[hbm] * 6,
         out_specs=(anywhere, anywhere),
         scratch_shapes=[
             pltpu.VMEM((rows, D), BF),
+            pltpu.VMEM((D, rows), BF),
             pltpu.VMEM((D, D), BF),
             pltpu.VMEM((D, D), BF),
             pltpu.VMEM((2, 640), BF),
@@ -326,12 +335,11 @@
             pltpu.VMEM((3, 32, D), BF),
             pltpu.VMEM((3, 32, 128), F32),
             pltpu.VMEM(block, BF),
-            pltpu.VMEM((8,) + block, BF),
-            pltpu.VMEM((NY, 2, 32, D), BF),
-            pltpu.VMEM((NY, 2, 32, D), F32),
+            pltpu.VMEM((NY, 2) + block, BF),
+            pltpu.VMEM((NY, 32, D), BF),
+            pltpu.VMEM((NY, 32, D), F32),
             pltpu.VMEM((NY, 32, D), BF),
             pltpu.VMEM((NY, 32, D), BF),
-            pltpu.VMEM((NY, 32, D), F32),
             pltpu.VMEM((3, 32, D), BF),
             pltpu.VMEM(block, BF),
             dma((8,)), dma((16,)), dma((4,)), dma((4,)), dma((4,)),
@@ -341,9 +349,12 @@
             dma((Q, 4)), dma((Q,)), dma((Q, 3)), dma((Q, 3)), dma((Q, 4)), dma((Q, 4)),
         ],
         compiler_params=pltpu.CompilerParams(
-            collective_id=0, has_side_effects=True, vmem_limit_bytes=60 * 1024 * 1024
+            collective_id=0, has_side_effects=True, vmem_limit_bytes=48 * 1024 * 1024
         ),
-    )(tokens[0], slot_keys.T, w_in, b_in, w_out.reshape(-1, D), b_out)
+    )(*(
+        pltpu.with_memory_space_constraint(a, pltpu.HBM)
+        for a in (tokens[0], slot_keys.T, w_in, b_in, w_out.reshape(-1, D), b_out)
+    ))
     mixed = jnp.dot(comb, back.reshape(slots, D), preferred_element_type=F32)
     return mixed.astype(BF)[None]
 

time: 67.1 us -> 64 us (0.954)
  Pallas kernels: 63.2 us -> 61.4 us
  matrix products: 3.8 us -> 2.53 us
    pallas_call x1, Pallas kernels: 63.2 us -> 61.4 us  [on_device(): pl.pallas_call(kernel, out_shape=(pltpu.VMEM((rows, slots), BF), pltpu.VM...]
    dot_general x1, matrix products: 3.8 us -> 2.53 us  [on_device(): mixed = jnp.dot(comb, back.reshape(slots, D), preferred_element_type=F32)]
where the time goes in v3:
time: 64 us
  Pallas kernels  61.4 us (96%)
  matrix products  2.53 us (4%)
    pallas_call x1, Pallas kernels, on_device(): pl.pallas_call(kernel, out_shape=(pltpu.VMEM((rows, slots), BF), pltpu.VM...  61.4 us
    dot_general x1, matrix products, on_device(): mixed = jnp.dot(comb, back.reshape(slots, D), preferred_element_type=F32)  2.53 us

profile of v3, /device:TPU:1, one launch (start us, length us, event | category | flops | bytes accessed | tf_op | source)
XLA Modules:
  0.0 64.0 jit_solution(13031900542427393208)
XLA Ops:
  0.0 61.4 %shard_map.64 = (bf16[1152,256]{1,0:T(8,128)(2,1)S(1)}, bf16[4,2,4,8,1280]{4,3,2,1,0:T(8,128)(2,1)S(1)}) custom-call(bf16[1152,1280]{1,0:T(8,128)(2,1)} %bitcast.10, bf16[8,1280]{1,0:T(8,128)(2,1)} %bitcast.11, bf16[2,1280,640]{2,1,0:T(8,128)(2,1)} %win_hbm.1, bf16[2,640]{1,0:T(2,128)(2,1)} %bin_hbm.1, bf16[1280,1280]{1,0:T(8,128)(2,1)} %bitcast.9, ...), custom_call_target="tpu_custom_call" | custom-call | tf_op jit(solution)/shard_map/pallas_call | solution.py:309
  61.4 2.5 %fusion = bf16[1,1152,1280]{2,1,0:T(8,128)(2,1)} fusion(bf16[1152,256]{1,0:T(8,128)(2,1)S(1)} %get-tuple-element.7, bf16[256,1280]{1,0:T(8,128)(2,1)S(1)} %bitcast.8), kind=kOutput, calls=%fused_computation.1 | convolution fusion | flops 756449280 | bytes 4194304 | tf_op jit(solution)/shard_map/dot_general | solution.py:358

commit v4 on v3

--- a/solution.py
+++ b/solution.py
@@ -13,6 +13,7 @@
 D = 1280
 PARTS = ((0, 640), (640, 640))
 Q = len(PARTS)
+MIX_STEPS = 6
 
 
 def kernel(
@@ -65,15 +66,15 @@
 
         started.append((w_to, cp))
 
-    def drain():
-        for w_to, cp in started:
+    def drain(count):
+        for w_to, cp in started[:count]:
             if w_to is None:
                 cp.wait_send()
             else:
                 @pl.when(w_to != w)
                 def _():
                     cp.wait_send()
-        started.clear()
+        del started[:count]
 
     def wait_for(ref, sem):
         pltpu.make_async_copy(ref, ref, sem).wait()
@@ -86,9 +87,6 @@
             (wout_hbm, wout), (bin_hbm, b_in), (bout_hbm, b_out),
         ))
     ]
-    for cp in loads:
-        cp.start()
-
     barrier = pltpu.get_barrier_semaphore()
 
     def greet(w_to, n_to):
@@ -105,6 +103,8 @@
     for k in (2, 1, 3):
         greet(*y_peer(k))
     greet(*sib)
+    for cp in loads:
+        cp.start()
     pl.semaphore_wait(barrier, 20 - c)
     loads[0].wait()
 
@@ -206,6 +206,7 @@
         for k in range(NY):
             wait_for(place(lax.rem(y + NY - k, NY), 1 - c), s_recv.at[k])
 
+    before = len(started)
     for q, (at, size) in enumerate(PARTS):
         for k in (1, 3, 2):
             wait_for(far.at[k - 1, :, cols(q)], b_recv.at[q, k - 1])
@@ -216,7 +217,7 @@
         plane(
             lambda i: ready.at[i, :, cols(q)], slots_in.at[y, c, lax.rem(z, 4), :, cols(q)], c_send.at[q], c_recv.at[q]
         )
-    drain()
+    drain(before)
 
     def gather1(q):
         return (
@@ -256,6 +257,7 @@
         out = jnp.dot(hid_c, wout[:, cols(q)], preferred_element_type=F32)
         own_part[:, :, cols(q)] = out.reshape(NY, 32, size)
 
+    before = len(started)
     for q, (at, size) in enumerate(PARTS):
         wait_for(sib_part.at[:, :, cols(q)], f_recv.at[q])
         chip = own_part[:, :, cols(q)] + sib_part[:, :, cols(q)].astype(F32)
@@ -266,10 +268,11 @@
                 half2.at[lax.rem(y + k, NY), :, cols(q)], far2.at[k - 1, :, cols(q)],
                 g_send.at[q, k - 1], g_recv.at[q, k - 1], y_peer(k),
             )
-    drain()
+    drain(before)
     bias = b_out[...].astype(F32)
     first = lax.rem(lax.broadcasted_iota(jnp.int32, (32, 1), 0), OWN) < 4
     bias = jnp.where(first, bias[0:1], bias[1:2])
+    before = len(started)
     for q, (at, size) in enumerate(PARTS):
         for k in (1, 3, 2):
             wait_for(far2.at[k - 1, :, cols(q)], g_recv.at[q, k - 1])
@@ -280,7 +283,7 @@
         plane(
             lambda i: ready2.at[i, :, cols(q)], back.at[x, z // 4, lax.rem(z, 4), :, cols(q)], i_send.at[q], i_recv.at[q]
         )
-    drain()
+    drain(before)
 
     def gather2(q):
         return (
@@ -292,11 +295,26 @@
         wait_for(back.at[gx, h, :, :, cols(q)], i_recv.at[q])
         gather_start(*gather2(q))
     comb_out.wait()
+    before = len(started)
     for q in range(Q):
         gather_forward(*gather2(q))
+    drain(before)
     for q in range(Q):
         gather_end(*gather2(q))
-    drain()
+    drain(len(started))
+
+
+def mix(comb, slot_out, out_ref, out, sem):
+    step = out.shape[0] // MIX_STEPS
+    copies = []
+    for i in range(MIX_STEPS):
+        rows = pl.ds(i * step, step)
+        out[rows, :] = jnp.dot(comb[rows, :], slot_out[...], preferred_element_type=F32).astype(BF)
+        cp = pltpu.make_async_copy(out.at[rows], out_ref.at[rows], sem.at[i])
+        cp.start()
+        copies.append(cp)
+    for cp in copies:
+        cp.wait()
 
 
 def on_device(tokens, slot_keys, w_in, b_in, w_out, b_out):
@@ -355,8 +373,18 @@
         pltpu.with_memory_space_constraint(a, pltpu.HBM)
         for a in (tokens[0], slot_keys.T, w_in, b_in, w_out.reshape(-1, D), b_out)
     ))
-    mixed = jnp.dot(comb, back.reshape(slots, D), preferred_element_type=F32)
-    return mixed.astype(BF)[None]
+    vmem = pl.BlockSpec(memory_space=pltpu.VMEM)
+    return pl.pallas_call(
+        mix,
+        out_shape=jax.ShapeDtypeStruct((rows, D), BF),
+        in_specs=[vmem, vmem],
+        out_specs=anywhere,
+        scratch_shapes=[pltpu.VMEM((rows, D), BF), dma((MIX_STEPS,))],
+        compiler_params=pltpu.CompilerParams(vmem_limit_bytes=32 * 1024 * 1024),
+    )(
+        pltpu.with_memory_space_constraint(comb, pltpu.VMEM),
+        pltpu.with_memory_space_constraint(back.reshape(slots, D), pltpu.VMEM),
+    )[None]
 
 
 def solution(mesh):

time: 64 us -> 63.4 us (level)
  matrix products: 2.53 us -> 0 us
  Pallas kernels: 61.4 us -> 63.3 us
    dot_general x1 -> x0, matrix products: 2.53 us -> none  [on_device(): mixed = jnp.dot(comb, back.reshape(slots, D), preferred_element_type=F32)]
    pallas_call x0 -> x1, Pallas kernels: none -> 1.97 us  [on_device(): pl.pallas_call(mix, out_shape=jax.ShapeDtypeStruct((rows, D), BF), in_spe...]
where the time goes in v4:
time: 63.4 us; the launch traced here: 63.3 us
  Pallas kernels  63.3 us (100%)
    pallas_call x1, Pallas kernels, on_device(): pl.pallas_call(kernel, out_shape=(pltpu.VMEM((rows, slots), BF), pltpu.VM...  61.4 us
    pallas_call x1, Pallas kernels, on_device(): pl.pallas_call(mix, out_shape=jax.ShapeDtypeStruct((rows, D), BF), in_spe...  1.97 us

profile of v4, /device:TPU:1, one launch (start us, length us, event | category | flops | bytes accessed | tf_op | source)
XLA Modules:
  0.0 63.3 jit_solution(13748741670155052944)
XLA Ops:
  0.0 61.4 %shard_map.64 = (bf16[1152,256]{1,0:T(8,128)(2,1)S(1)}, bf16[4,2,4,8,1280]{4,3,2,1,0:T(8,128)(2,1)S(1)}) custom-call(bf16[1152,1280]{1,0:T(8,128)(2,1)} %bitcast.7, bf16[8,1280]{1,0:T(8,128)(2,1)} %bitcast.8, bf16[2,1280,640]{2,1,0:T(8,128)(2,1)} %win_hbm.1, bf16[2,640]{1,0:T(2,128)(2,1)} %bin_hbm.1, bf16[1280,1280]{1,0:T(8,128)(2,1)} %bitcast.6, ...), custom_call_target="tpu_custom_call" | custom-call | tf_op jit(solution)/shard_map/pallas_call | solution.py:327
  61.4 2.0 %shard_map.65 = bf16[1152,1280]{1,0:T(8,128)(2,1)} custom-call(bf16[1152,256]{1,0:T(8,128)(2,1)S(1)} %get-tuple-element.7.comb, bf16[256,1280]{1,0:T(8,128)(2,1)S(1)} %bitcast.5), custom_call_target="tpu_custom_call" | custom-call | tf_op jit(solution)/shard_map/pallas_call | solution.py:377

commit v5 on v4

--- a/solution.py
+++ b/solution.py
@@ -235,9 +235,10 @@
     first = lax.rem(lax.broadcasted_iota(jnp.int32, (128, 1), 0), OWN) < 4
     bias = b_in[...].astype(F32)
 
-    def hidden(core):
+    def hidden(core, arrive=lambda q: None):
         hid = None
         for q, (at, size) in enumerate(PARTS):
+            arrive(q)
             rows_in = slots_in[:, core, :, :, cols(q)].reshape(128, size)
             term = jnp.dot(rows_in, win[cols(q), :], preferred_element_type=F32)
             hid = term if hid is None else hid + term
@@ -246,9 +247,7 @@
         return jnp.concatenate((jnp.where(first, hid, 0.0).astype(BF), jnp.where(first, 0.0, hid).astype(BF)), axis=1)
 
     hid_c = hidden(c)
-    for q in range(Q):
-        gather_end(*gather1(q))
-    hid_sib = hidden(1 - c)
+    hid_sib = hidden(1 - c, lambda q: gather_end(*gather1(q)))
     for q, (at, size) in enumerate(PARTS):
         out = jnp.dot(hid_sib, wout[:, cols(q)], preferred_element_type=F32)
         part[:, :, cols(q)] = out.astype(BF).reshape(NY, 32, size)

time: 63.4 us -> 63.4 us (level)
  no operation moved by 1% of the time
where the time goes in v5:
time: 63.4 us; the launch traced here: 63.3 us
  Pallas kernels  63.3 us (100%)
    pallas_call x1, Pallas kernels, on_device(): pl.pallas_call(kernel, out_shape=(pltpu.VMEM((rows, slots), BF), pltpu.VM...  61.3 us
    pallas_call x1, Pallas kernels, on_device(): pl.pallas_call(mix, out_shape=jax.ShapeDtypeStruct((rows, D), BF), in_spe...  1.97 us

profile of v5, /device:TPU:1, one launch (start us, length us, event | category | flops | bytes accessed | tf_op | source)
XLA Modules:
  0.0 63.3 jit_solution(8643511426116856949)
XLA Ops:
  0.0 61.3 %shard_map.64 = (bf16[1152,256]{1,0:T(8,128)(2,1)S(1)}, bf16[4,2,4,8,1280]{4,3,2,1,0:T(8,128)(2,1)S(1)}) custom-call(bf16[1152,1280]{1,0:T(8,128)(2,1)} %bitcast.7, bf16[8,1280]{1,0:T(8,128)(2,1)} %bitcast.8, bf16[2,1280,640]{2,1,0:T(8,128)(2,1)} %win_hbm.1, bf16[2,640]{1,0:T(2,128)(2,1)} %bin_hbm.1, bf16[1280,1280]{1,0:T(8,128)(2,1)} %bitcast.6, ...), custom_call_target="tpu_custom_call" | custom-call | tf_op jit(solution)/shard_map/pallas_call | solution.py:326
  61.3 2.0 %shard_map.65 = bf16[1152,1280]{1,0:T(8,128)(2,1)} custom-call(bf16[1152,256]{1,0:T(8,128)(2,1)S(1)} %get-tuple-element.7.comb, bf16[256,1280]{1,0:T(8,128)(2,1)S(1)} %bitcast.5), custom_call_target="tpu_custom_call" | custom-call | tf_op jit(solution)/shard_map/pallas_call | solution.py:376
